TPU v7x, 128 devices: a whole 4x4x4 slice. The times are simulated.
128 devices in a mesh: comp: 4 (over y), lon: 32 (over x, z, core).
Axes of the slice: x: 4, y: 4, z: 4, core: 2. Of those that a mesh axis runs over, the one named last changes fastest.
Arguments:
- spectra: float32 [384, 1728, 128], P(('comp', 'lon')), may hold values from 0.05 to 2
- wind_vectors: float32 [384, 2, 128], P(('comp', 'lon')), may hold values from -30 to 30
- slot_block: int32 [384], replicated, may hold values from -1 to 7, as said below
- wet_mask: int32 [128, 256], replicated, may hold values 0 or 1
- depth_class: int32 [128, 2], replicated, may hold values from 0 to 7
Outputs:
- new_spectra: float32 [384, 1728, 128], P(('comp', 'lon'))
Inputs may be any that keep to these rules, and one draw needn't show every extreme that they name: `slot_block`: slot k of device c * 32 + r (comp index c, lon index r) holds block v of region (r + k - 1) mod 32, at longitude region * 4 + v // 2 and latitude block v mod 2, or is empty (-1); each of a region's 8 blocks is held by exactly one slot, and each of the three bands k of every region holds at least one block.
All inputs are finite; a program needn't handle non-finite values.
Results may differ from a plain program's by a relative error of at most 0.00002.
Values sent between devices are 32-bit elements; how exact they have to be, the bound alone decides.
A program may use at most 128 MiB of HBM per device.

v0:
```python
import functools

import jax
import jax.numpy as jnp
import numpy as np
from jax import lax
from jax.experimental import pallas as pl
from jax.experimental.pallas import tpu as pltpu
from jax.sharding import PartitionSpec as P

MESH = pl.DeviceIdType.MESH

DIRS = 36
HALF = DIRS // 2
FREQS = 48
GROUPS = 4
REGIONS = 32
SLOTS = 3
SOURCES = GROUPS * SLOTS
POINTS = 128
NDEPTH = 8
NSUB = 4
BLOCKS = 8
GRID_LON = 128
REGION_LONS = GRID_LON // REGIONS
GROUP_FREQS = FREQS // GROUPS
COMPS = FREQS * DIRS
GROUP_COMPS = GROUP_FREQS * DIRS

CHUNK = 2
CHUNKS = GROUP_FREQS // CHUNK
ROWS = CHUNK * DIRS

GRAVITY = 9.81

ORDER = [(q + 27) % DIRS for q in range(DIRS)]
ANGLE = (np.arange(DIRS) + 0.5) * (2.0 * np.pi / DIRS)
COS = np.cos(ANGLE)
SIN = np.sin(ANGLE)
COS_FACE = 0.5 * (COS + np.roll(COS, -1))
SIN_FACE = 0.5 * (SIN + np.roll(SIN, -1))

T_SPEED = 0
T_ALONG = T_SPEED + NDEPTH * FREQS
T_GAIN = T_ALONG + FREQS
T_SQUARE = T_GAIN + FREQS
T_WEIGHT = T_SQUARE + FREQS
T_WEIGHT_FREQ = T_WEIGHT + FREQS
T_SIZE = 640


def scalar_table():
    sigma = 2.0 * np.pi * 0.0418 * 1.07 ** np.arange(FREQS, dtype=np.float64)
    depth = 8.0 * 2.0 ** np.arange(NDEPTH, dtype=np.float64)
    deep = sigma * sigma / GRAVITY
    number = deep[None, :] / np.sqrt(np.tanh(deep[None, :] * depth[:, None]))
    twice = 2.0 * number * depth[:, None]
    factor = 2.0 * twice * np.exp(-twice) / (1.0 - np.exp(-2.0 * twice))
    speed = 0.5 * sigma[None, :] / number * (1.0 + factor)
    speed = speed / speed.max()
    weight = sigma / (sigma.sum() * DIRS)
    table = np.zeros(T_SIZE, np.float64)
    table[T_SPEED:T_ALONG] = speed.reshape(-1)
    table[T_ALONG:T_GAIN] = sigma / GRAVITY
    table[T_GAIN:T_SQUARE] = 0.5 * sigma / sigma[-1]
    table[T_SQUARE:T_WEIGHT] = sigma * sigma
    table[T_WEIGHT:T_WEIGHT_FREQ] = weight
    table[T_WEIGHT_FREQ:T_WEIGHT_FREQ + FREQS] = weight * sigma
    return table.astype(np.float32)


def latitude_table():
    count = 2 * POINTS
    phi = (-60.0 + (np.arange(count) + 0.5) * 120.0 / count) * np.pi / 180.0
    rows = np.concatenate([0.5 * 0.45 / np.cos(phi), 0.3 * np.tan(phi)])
    parts = rows.reshape(2, 1, 2, POINTS)
    return np.broadcast_to(parts, (2, REGION_LONS, 2, POINTS)).reshape(2, 8, POINTS).astype(np.float32)


def wait_bytes(ref, sem):
    pltpu.make_async_copy(ref, ref, sem).wait()


def kernel(
    x, wind, slots, wet, depth, table, lat, out,
    xv, windv, slot_s, wetv, depthv, table_s, latv,
    aux_out, aux_in, scal, near, coef, ordered, field, halo_w, halo_e, back, blocks, outb,
    local_sem, in_send, in_recv, aux_send, aux_recv, halo_send, halo_recv, out_send, out_recv,
    *inb,
):
    me_c = lax.axis_index("comp")
    me_r = lax.axis_index("lon")

    def region(shift):
        return lax.rem(me_r + (shift + REGIONS), REGIONS)

    loads = [
        pltpu.make_async_copy(src, dst, local_sem.at[n])
        for n, (src, dst) in enumerate(
            ((x, xv), (wind, windv), (slots, slot_s), (wet, wetv), (depth, depthv), (table, table_s), (lat, latv))
        )
    ]
    for load in loads:
        load.start()

    barrier = pltpu.get_barrier_semaphore()
    for dg in range(GROUPS):
        for dr in (-1, 0, 1):
            if dg or dr:
                pl.semaphore_signal(
                    barrier, inc=1, device_id=(lax.rem(me_c + dg, GROUPS), region(dr)), device_id_type=MESH
                )
    pl.semaphore_wait(barrier, SOURCES - 1)

    for ch in range(CHUNKS):
        for dg in (2, 1, 3, 0):
            to = lax.rem(me_c + dg, GROUPS)
            for k in range(SLOTS):
                src = x.at[k, pl.ds(to * GROUP_COMPS + ch * ROWS, ROWS)]
                dst = inb[ch].at[me_c * SLOTS + k]
                if dg == 0 and k == 1:
                    pltpu.make_async_copy(src, dst, in_recv.at[ch]).start()
                else:
                    pltpu.make_async_remote_copy(
                        src, dst, in_send.at[ch], in_recv.at[ch], device_id=(to, region(k - 1)), device_id_type=MESH
                    ).start()

    row = lax.broadcasted_iota(jnp.int32, (8, POINTS), 0)
    lane = lax.broadcasted_iota(jnp.int32, (8, POINTS), 1)

    for load in loads:
        load.wait()
    upper = row < 4
    for k in range(SLOTS):
        def pair(p, sums, k=k):
            total, moment = sums
            tiles = [xv[k, pl.ds(pl.multiple_of(p * 72 + 8 * n, 8), 8), :] for n in range(9)]
            first = (tiles[0] + tiles[1]) + (tiles[2] + tiles[3]) + jnp.where(upper, tiles[4], 0.0)
            second = (tiles[5] + tiles[6]) + (tiles[7] + tiles[8]) + jnp.where(upper, 0.0, tiles[4])
            total = total + first * table_s[T_WEIGHT + 2 * p] + second * table_s[T_WEIGHT + 2 * p + 1]
            moment = moment + first * table_s[T_WEIGHT_FREQ + 2 * p] + second * table_s[T_WEIGHT_FREQ + 2 * p + 1]
            return total, moment

        zero = jnp.zeros((8, POINTS), jnp.float32)
        total, moment = lax.fori_loop(0, FREQS // 2, pair, (zero, zero))
        total = jnp.sum(total, axis=0, keepdims=True)
        moment = jnp.sum(moment, axis=0, keepdims=True)
        mean = moment / (total + 1e-6)
        aux_out[k] = zero
        aux_out[k, 0:2, :] = windv[k]
        aux_out[k, 2:3, :] = 0.3 * (total / (total + 1.0)) / (mean * mean)

    for dg in (2, 1, 3, 0):
        to = lax.rem(me_c + dg, GROUPS)
        for k in range(SLOTS):
            dst = aux_in.at[me_c * SLOTS + k]
            if dg == 0 and k == 1:
                pltpu.make_async_copy(aux_out.at[k], dst, aux_recv).start()
            else:
                pltpu.make_async_remote_copy(
                    aux_out.at[k], dst, aux_send, aux_recv, device_id=(to, region(k - 1)), device_id_type=MESH
                ).start()

    for n in range(3):
        for v in range(BLOCKS):
            lon = lax.rem(me_r * REGION_LONS + (v // 2 + n - 1 + GRID_LON), GRID_LON)
            part = v % 2
            rows = pl.ds(pl.multiple_of(lon // 8 * 8, 8), 8)
            here = row == lax.rem(lon, 8)
            levels = jnp.broadcast_to(depthv[rows, part:part + 1].astype(jnp.float32), (8, POINTS))
            near[0, n, v:v + 1, :] = jnp.sum(jnp.where(here, levels, 0.0), axis=0, keepdims=True)
            cells = wetv[rows, part * POINTS:(part + 1) * POINTS].astype(jnp.float32)
            near[1, n, v:v + 1, :] = jnp.sum(jnp.where(here, cells, 0.0), axis=0, keepdims=True)

    def shift_down(value):
        rolled = pltpu.roll(value, 1, 1)
        return jnp.where(lane == 0, pltpu.roll(rolled, 1, 0), rolled)

    def shift_up(value):
        rolled = pltpu.roll(value, POINTS - 1, 1)
        return jnp.where(lane == POINTS - 1, pltpu.roll(rolled, 7, 0), rolled)

    def prepare(i, _):
        speeds = []
        for n in range(3):
            level = near[0, n]
            speed = jnp.zeros((8, POINTS), jnp.float32)
            for d in range(NDEPTH):
                speed = jnp.where(level == float(d), table_s[T_SPEED + d * FREQS + me_c * GROUP_FREQS + i], speed)
            speeds.append(speed)
        west, mid, east = speeds
        wet_west, wet_mid, wet_east = near[1, 0], near[1, 1], near[1, 2]
        coef[i, 0] = latv[0] * (mid + east) * wet_mid * wet_east
        coef[i, 1] = latv[0] * (mid + west) * wet_mid * wet_west
        last = (lax.rem(row, 2) == 1) & (lane == POINTS - 1)
        face = jnp.where(last, 0.0, 0.45 * (mid + shift_up(mid)) * wet_mid * shift_up(wet_mid))
        coef[i, 2] = face
        coef[i, 3] = shift_down(face)
        coef[i, 4] = latv[1] * mid
        coef[i, 5] = 0.4 * (east - west)
        return 0

    lax.fori_loop(0, GROUP_FREQS, prepare, 0)

    held = []
    for s in range(SOURCES):
        held.append(slot_s[((s // SLOTS) * REGIONS + region(1 - s % SLOTS)) * SLOTS + s % SLOTS])
    holder = []
    for v in range(BLOCKS):
        found = jnp.int32(0)
        for s in range(SOURCES):
            found = jnp.where(held[s] == v, jnp.int32(s), found)
        holder.append(found)
    back_row = [jnp.maximum(h, 0) for h in held]

    wait_bytes(aux_in, aux_recv)
    for v in range(BLOCKS):
        for n in range(3):
            scal[n, v:v + 1, :] = aux_in[holder[v]][n:n + 1, :]

    def halo_copies(ch, s):
        freqs = pl.ds(ch * CHUNK, CHUNK)
        return (
            pltpu.make_async_remote_copy(
                field.at[s, freqs, 0:HALF, 6:8, :], halo_w.at[s, freqs, :, 0:2, :],
                halo_send.at[0, s, ch], halo_recv.at[0, s, ch], device_id=(me_c, region(1)), device_id_type=MESH,
            ),
            pltpu.make_async_remote_copy(
                field.at[s, freqs, HALF:DIRS, 0:2, :], halo_e.at[s, freqs, :, 6:8, :],
                halo_send.at[1, s, ch], halo_recv.at[1, s, ch], device_id=(me_c, region(-1)), device_id_type=MESH,
            ),
        )

    def send_halos(ch, s):
        for copy in halo_copies(ch, s):
            copy.start()

    def source_terms(ch):
        wind_x, wind_y, damp = scal[0], scal[1], scal[2]
        for n in range(CHUNK):
            i = ch * CHUNK + n
            f = me_c * GROUP_FREQS + i
            along = table_s[T_ALONG + f]
            gain = table_s[T_GAIN + f]
            scale = 1.0 / (1.0 + damp * table_s[T_SQUARE + f])
            for q in range(DIRS):
                j = ORDER[q]
                energy = ordered[pl.ds(n * DIRS + j, 8, stride=ROWS), :]
                ratio = jnp.maximum((wind_x * float(COS[j]) + wind_y * float(SIN[j])) * along, 1.0)
                field[0, i, q] = energy * ((1.0 + gain) - gain / ratio) * scale

    def substep(ch, s):
        def one(n, _):
            i = ch * CHUNK + n
            east_face, west_face, up_face, down_face = coef[i, 0], coef[i, 1], coef[i, 2], coef[i, 3]
            turn_lat, turn_depth = coef[i, 4], coef[i, 5]
            wet_here = near[1, 1]

            def moved(q):
                j = ORDER[q]
                energy = field[s, i, q]
                if q < HALF:
                    west = jnp.where(row < 2, halo_w[s, i, q], pltpu.roll(energy, 2, 0))
                    flux = east_face * energy - west_face * west
                else:
                    east = jnp.where(row >= 6, halo_e[s, i, q - HALF], pltpu.roll(energy, 6, 0))
                    flux = east_face * east - west_face * energy
                energy = energy - float(COS[j]) * flux
                if SIN[j] > 0:
                    share = up_face * energy
                    flux = share - shift_down(share)
                else:
                    share = down_face * energy
                    flux = shift_up(share) - share
                return energy - float(SIN[j]) * flux

            def turned(q, here, following):
                j = ORDER[q]
                rate = turn_lat * float(COS_FACE[j]) + turn_depth * float(SIN_FACE[j])
                return rate * jnp.where(rate > 0.0, here, following)

            energies = [moved(q) for q in range(DIRS)]
            fluxes = [turned(q, energies[q], energies[(q + 1) % DIRS]) for q in range(DIRS)]
            for q in range(DIRS):
                field[s + 1, i, q] = (energies[q] - (fluxes[q] - fluxes[q - 1])) * wet_here
            return 0

        lax.fori_loop(0, CHUNK, one, 0)

    def send_back(ch):
        for n in range(CHUNK):
            for q in range(DIRS):
                back[pl.ds(n * DIRS + ORDER[q], 8, stride=ROWS), :] = field[NSUB, ch * CHUNK + n, q]
        for v in range(BLOCKS):
            blocks[v] = back[v * ROWS:(v + 1) * ROWS, :]
        for s in range(SOURCES):
            outb[ch, s] = blocks[back_row[s]]
        for dg in (2, 1, 3, 0):
            to = lax.rem(me_c + dg, GROUPS)
            for k in range(SLOTS):
                src = outb.at[ch, to * SLOTS + k]
                dst = out.at[k, pl.ds(me_c * GROUP_COMPS + ch * ROWS, ROWS)]
                if dg == 0 and k == 1:
                    pltpu.make_async_copy(src, dst, out_recv).start()
                else:
                    pltpu.make_async_remote_copy(
                        src, dst, out_send.at[ch], out_recv, device_id=(to, region(1 - k)), device_id_type=MESH
                    ).start()

    def step(t, _):
        def one(n, _):
            s = NSUB - 1 - n
            ch = t - 1 - s

            @pl.when((ch >= 0) & (ch < CHUNKS))
            def _():
                for copy in halo_copies(ch, s):
                    copy.wait_recv()
                substep(ch, s)

                @pl.when(s < NSUB - 1)
                def _():
                    send_halos(ch, s + 1)

                @pl.when(s == NSUB - 1)
                def _():
                    send_back(ch)

            return 0

        lax.fori_loop(0, NSUB, one, 0)

        for ch in range(CHUNKS):
            @pl.when(t == ch)
            def _(ch=ch):
                wait_bytes(inb[ch], in_recv.at[ch])
                for v in range(BLOCKS):
                    ordered[v * ROWS:(v + 1) * ROWS, :] = inb[ch][holder[v]]

        @pl.when(t < CHUNKS)
        def _():
            source_terms(t)
            send_halos(t, 0)

        return 0

    lax.fori_loop(0, CHUNKS + NSUB, step, 0)

    wait_bytes(aux_in.at[0:SOURCES - 1], aux_send)
    for ch in range(CHUNKS):
        wait_bytes(inb[ch].at[0:SOURCES - 1], in_send.at[ch])
        wait_bytes(outb.at[ch, 0:SOURCES - 1], out_send.at[ch])

    def drain(n, _):
        for copy in halo_copies(lax.rem(n, CHUNKS), n // CHUNKS):
            copy.wait_send()
        return 0

    lax.fori_loop(0, CHUNKS * NSUB, drain, 0)
    wait_bytes(out, out_recv)


def per_device(spectra, wind_vectors, slot_block, wet_mask, depth_class):
    hbm = pl.BlockSpec(memory_space=pltpu.HBM)
    f32 = jnp.float32
    dma = pltpu.SemaphoreType.DMA
    moved = pl.pallas_call(
        kernel,
        out_shape=jax.ShapeDtypeStruct((SLOTS, COMPS, POINTS), f32),
        in_specs=[hbm] * 7,
        out_specs=hbm,
        scratch_shapes=[
            pltpu.VMEM((SLOTS, COMPS, POINTS), f32),
            pltpu.VMEM((SLOTS, 2, POINTS), f32),
            pltpu.SMEM((GROUPS * REGIONS * SLOTS,), jnp.int32),
            pltpu.VMEM((GRID_LON, 2 * POINTS), jnp.int32),
            pltpu.VMEM((GRID_LON, 2), jnp.int32),
            pltpu.SMEM((T_SIZE,), f32),
            pltpu.VMEM((2, 8, POINTS), f32),
            pltpu.VMEM((SLOTS, 8, POINTS), f32),
            pltpu.VMEM((SOURCES, 8, POINTS), f32),
            pltpu.VMEM((3, 8, POINTS), f32),
            pltpu.VMEM((2, 3, 8, POINTS), f32),
            pltpu.VMEM((GROUP_FREQS, 6, 8, POINTS), f32),
            pltpu.VMEM((BLOCKS * ROWS, POINTS), f32),
            pltpu.VMEM((NSUB + 1, GROUP_FREQS, DIRS, 8, POINTS), f32),
            pltpu.VMEM((NSUB, GROUP_FREQS, HALF, 8, POINTS), f32),
            pltpu.VMEM((NSUB, GROUP_FREQS, HALF, 8, POINTS), f32),
            pltpu.VMEM((BLOCKS * ROWS, POINTS), f32),
            pltpu.VMEM((BLOCKS, ROWS, POINTS), f32),
            pltpu.VMEM((CHUNKS, SOURCES, ROWS, POINTS), f32),
            dma((7,)),
            dma((CHUNKS,)),
            dma((CHUNKS,)),
            dma,
            dma,
            dma((2, NSUB, CHUNKS)),
            dma((2, NSUB, CHUNKS)),
            dma((CHUNKS,)),
            dma,
        ] + [pltpu.VMEM((SOURCES, ROWS, POINTS), f32) for _ in range(CHUNKS)],
        compiler_params=pltpu.CompilerParams(
            collective_id=0, has_side_effects=True, vmem_limit_bytes=62 * 1024 * 1024
        ),
        name="wave_step",
    )(spectra, wind_vectors, slot_block, wet_mask, depth_class, scalar_table(), latitude_table())
    first = (lax.axis_index("comp") * REGIONS + lax.axis_index("lon")) * SLOTS
    mine = lax.dynamic_slice_in_dim(slot_block, first, SLOTS)
    return jnp.where(mine[:, None, None] >= 0, moved, 0.0)


def solution(mesh):
    return jax.shard_map(
        per_device,
        mesh=mesh,
        in_specs=(P(("comp", "lon"), None, None), P(("comp", "lon"), None, None), P(), P(), P()),
        out_specs=P(("comp", "lon"), None, None),
        check_vma=False,
    )
```

profile of v0, /device:TPU:1, one launch (start us, length us, event | category | flops | bytes accessed | tf_op | source)
XLA Modules:
  0.0 102.8 jit_solution(13439150147217088727)
XLA Ops:
  0.0 1.4 %copy.8.depth = s32[128,2]{1,0:T(8,128)} copy(s32[128,2]{0,1:T(2,128)} %param.11) | data formatting | bytes 2048 | tf_op args[4]
  1.4 97.1 %wave_step.1 = f32[3,1728,128]{2,1,0:T(8,128)} custom-call(f32[3,1728,128]{2,1,0:T(8,128)} %x.1, f32[3,2,128]{2,1,0:T(2,128)} %wind.1, s32[384]{0:T(512)} %slots.1, s32[128,256]{1,0:T(8,128)} %wet.1, s32[128,2]{1,0:T(8,128)} %copy.8.depth, f32[640]{0:T(1024)} %constant.24.clone.table, f32[2,8,128]{2,1,0:T(8,128)} %constant.25.clone.lat), custom_call_target="tpu_custom_call" | custom-call | tf_op jit(solution)/shard_map/wave_step/pallas_call | solution.py:367
  98.5 0.8 dynamic-slice_compare_fusion
  99.3 3.5 %broadcast_select_fusion = f32[3,1728,128]{2,1,0:T(8,128)} fusion(f32[3,1728,128]{2,1,0:T(8,128)} %wave_step.1, pred[3]{0:T(512)(128)(4,1)S(1)} %dynamic-slice_compare_fusion), kind=kLoop, calls=%fused_computation | loop fusion | flops 663552 | bytes 5308419 | tf_op jit(solution)/shard_map/jit(_where)/select_n | solution.py:409
where the time goes:
time: 103 us
  Pallas kernels  97.1 us (94%)
  other arithmetic  4.25 us (4%)
  local copies, waits for them, and re-layouts  1.41 us (1%)
    pallas_call x1, Pallas kernels, per_device(): pl.pallas_call(kernel, out_shape=jax.ShapeDtypeStruct((SLOTS, COMPS, POIN...  97.1 us
    select_n x1, other arithmetic, per_device(): return jnp.where(mine[:, None, None] >= 0, moved, 0.0)  3.49 us

commit v1 on v0

--- a/solution.py
+++ b/solution.py
@@ -47,6 +47,8 @@
 T_WEIGHT = T_SQUARE + FREQS
 T_WEIGHT_FREQ = T_WEIGHT + FREQS
 T_SIZE = 640
+
+WEST, MID, EAST, BESIDE = range(4)
 
 
 def scalar_table():
@@ -84,7 +86,7 @@
 def kernel(
     x, wind, slots, wet, depth, table, lat, out,
     xv, windv, slot_s, wetv, depthv, table_s, latv,
-    aux_out, aux_in, scal, near, coef, ordered, field, halo_w, halo_e, back, blocks, outb,
+    aux_out, aux_in, scal, cells, speeds, coef, ordered, field, halo_w, halo_e, one_on, two_on, three_on, back, blocks, outb,
     local_sem, in_send, in_recv, aux_send, aux_recv, halo_send, halo_recv, out_send, out_recv,
     *inb,
 ):
@@ -161,16 +163,20 @@
                     aux_out.at[k], dst, aux_send, aux_recv, device_id=(to, region(k - 1)), device_id_type=MESH
                 ).start()
 
-    for n in range(3):
-        for v in range(BLOCKS):
-            lon = lax.rem(me_r * REGION_LONS + (v // 2 + n - 1 + GRID_LON), GRID_LON)
-            part = v % 2
-            rows = pl.ds(pl.multiple_of(lon // 8 * 8, 8), 8)
-            here = row == lax.rem(lon, 8)
-            levels = jnp.broadcast_to(depthv[rows, part:part + 1].astype(jnp.float32), (8, POINTS))
-            near[0, n, v:v + 1, :] = jnp.sum(jnp.where(here, levels, 0.0), axis=0, keepdims=True)
-            cells = wetv[rows, part * POINTS:(part + 1) * POINTS].astype(jnp.float32)
-            near[1, n, v:v + 1, :] = jnp.sum(jnp.where(here, cells, 0.0), axis=0, keepdims=True)
+    for n in range(16):
+        lon = lax.rem(me_r * REGION_LONS + (n - 6 + GRID_LON), GRID_LON)
+        levels = jnp.where(lane[0:2] == lon, depthv[...].astype(jnp.float32), 0.0)
+        cells[0, 2 * n:2 * n + 2, :] = jnp.broadcast_to(jnp.sum(levels, axis=1, keepdims=True), (2, POINTS))
+        rows = pl.ds(pl.multiple_of(lon // 8 * 8, 8), 8)
+        here = row == lax.rem(lon, 8)
+        for part in range(2):
+            wet_rows = wetv[rows, part * POINTS:(part + 1) * POINTS].astype(jnp.float32)
+            cells[1, 2 * n + part:2 * n + part + 1, :] = jnp.sum(
+                jnp.where(here, wet_rows, 0.0), axis=0, keepdims=True
+            )
+
+    def from_lon(values, start):
+        return values[2 * (start + 6):2 * (start + 6) + 8]
 
     def shift_down(value):
         rolled = pltpu.roll(value, 1, 1)
@@ -180,24 +186,33 @@
         rolled = pltpu.roll(value, POINTS - 1, 1)
         return jnp.where(lane == POINTS - 1, pltpu.roll(rolled, 7, 0), rolled)
 
+    last = (lax.rem(row, 2) == 1) & (lane == POINTS - 1)
+    wets = cells.at[1]
+
     def prepare(i, _):
-        speeds = []
-        for n in range(3):
-            level = near[0, n]
+        for m in range(4):
+            level = cells[0, 8 * m:8 * m + 8]
             speed = jnp.zeros((8, POINTS), jnp.float32)
             for d in range(NDEPTH):
                 speed = jnp.where(level == float(d), table_s[T_SPEED + d * FREQS + me_c * GROUP_FREQS + i], speed)
-            speeds.append(speed)
-        west, mid, east = speeds
-        wet_west, wet_mid, wet_east = near[1, 0], near[1, 1], near[1, 2]
-        coef[i, 0] = latv[0] * (mid + east) * wet_mid * wet_east
-        coef[i, 1] = latv[0] * (mid + west) * wet_mid * wet_west
-        last = (lax.rem(row, 2) == 1) & (lane == POINTS - 1)
-        face = jnp.where(last, 0.0, 0.45 * (mid + shift_up(mid)) * wet_mid * shift_up(wet_mid))
-        coef[i, 2] = face
-        coef[i, 3] = shift_down(face)
-        coef[i, 4] = latv[1] * mid
-        coef[i, 5] = 0.4 * (east - west)
+            speeds[8 * m:8 * m + 8] = speed
+        made = []
+        for part, start in enumerate((-REGION_LONS, 0, REGION_LONS)):
+            west, mid, east = (from_lon(speeds, start + n) for n in (-1, 0, 1))
+            wet_west, wet_mid, wet_east = (from_lon(wets, start + n) for n in (-1, 0, 1))
+            face = jnp.where(last, 0.0, 0.45 * (mid + shift_up(mid)) * wet_mid * shift_up(wet_mid))
+            made.append((
+                latv[0] * (mid + east) * wet_mid * wet_east,
+                latv[0] * (mid + west) * wet_mid * wet_west,
+                face,
+                shift_down(face),
+                latv[1] * mid,
+                0.4 * (east - west),
+            ))
+        for n in range(6):
+            for part in range(3):
+                coef[i, part, n] = made[part][n]
+            coef[i, BESIDE, n] = jnp.where(row < 4, made[EAST][n], made[WEST][n])
         return 0
 
     lax.fori_loop(0, GROUP_FREQS, prepare, 0)
@@ -218,21 +233,18 @@
         for n in range(3):
             scal[n, v:v + 1, :] = aux_in[holder[v]][n:n + 1, :]
 
-    def halo_copies(ch, s):
+    def halo_copies(ch):
         freqs = pl.ds(ch * CHUNK, CHUNK)
-        return (
+        return [
             pltpu.make_async_remote_copy(
-                field.at[s, freqs, 0:HALF, 6:8, :], halo_w.at[s, freqs, :, 0:2, :],
-                halo_send.at[0, s, ch], halo_recv.at[0, s, ch], device_id=(me_c, region(1)), device_id_type=MESH,
-            ),
-            pltpu.make_async_remote_copy(
-                field.at[s, freqs, HALF:DIRS, 0:2, :], halo_e.at[s, freqs, :, 6:8, :],
-                halo_send.at[1, s, ch], halo_recv.at[1, s, ch], device_id=(me_c, region(-1)), device_id_type=MESH,
-            ),
-        )
-
-    def send_halos(ch, s):
-        for copy in halo_copies(ch, s):
+                field.at[freqs], halo.at[freqs], halo_send.at[n, ch], halo_recv.at[n, ch],
+                device_id=(me_c, region(shift)), device_id_type=MESH,
+            )
+            for n, (halo, shift) in enumerate(((halo_w, 1), (halo_e, -1)))
+        ]
+
+    def send_halos(ch):
+        for copy in halo_copies(ch):
             copy.start()
 
     def source_terms(ch):
@@ -247,50 +259,99 @@
                 j = ORDER[q]
                 energy = ordered[pl.ds(n * DIRS + j, 8, stride=ROWS), :]
                 ratio = jnp.maximum((wind_x * float(COS[j]) + wind_y * float(SIN[j])) * along, 1.0)
-                field[0, i, q] = energy * ((1.0 + gain) - gain / ratio) * scale
-
-    def substep(ch, s):
+                field[i, q] = energy * ((1.0 + gain) - gain / ratio) * scale
+
+    def along_lon(q, parts, coefs, ring):
+        turn = 2 if q < HALF else 6
+        rolled = [pltpu.roll(part, turn, 0) for part in parts]
+        edge = row < 2 if q < HALF else row >= 6
+        moved = []
+        for n, part in enumerate(parts):
+            other = n - 1 if q < HALF else n + 1
+            if ring:
+                beside = jnp.where(edge, rolled[other % len(parts)], rolled[n])
+            elif 0 <= other < len(parts):
+                beside = jnp.where(edge, rolled[other], rolled[n])
+            else:
+                beside = rolled[n]
+            from_west, from_east = (beside, part) if q < HALF else (part, beside)
+            flux = coefs[n][0] * from_east - coefs[n][1] * from_west
+            moved.append(part - float(COS[ORDER[q]]) * flux)
+        return moved
+
+    def along_lat(q, energy, coefs):
+        sine = float(SIN[ORDER[q]])
+        if sine > 0:
+            share = coefs[2] * energy
+            flux = share - shift_down(share)
+        else:
+            share = coefs[3] * energy
+            flux = shift_up(share) - share
+        return energy - sine * flux
+
+    def refracted(moved, coefs, store):
+        first = moved(0)
+        here = first
+        opening = before = None
+        for q in range(DIRS):
+            following = moved(q + 1) if q + 1 < DIRS else first
+            j = ORDER[q]
+            fluxes = []
+            for n, part in enumerate(here):
+                rate = coefs[n][4] * float(COS_FACE[j]) + coefs[n][5] * float(SIN_FACE[j])
+                fluxes.append(rate * jnp.where(rate > 0.0, part, following[n]))
+            if q == 0:
+                opening = fluxes
+            else:
+                for n, part in enumerate(here):
+                    store(q, n, part - (fluxes[n] - before[n]))
+            before = fluxes
+            here = following
+        for n, part in enumerate(first):
+            store(0, n, part - (opening[n] - before[n]))
+
+    def propagate(ch):
         def one(n, _):
             i = ch * CHUNK + n
-            east_face, west_face, up_face, down_face = coef[i, 0], coef[i, 1], coef[i, 2], coef[i, 3]
-            turn_lat, turn_depth = coef[i, 4], coef[i, 5]
-            wet_here = near[1, 1]
-
-            def moved(q):
-                j = ORDER[q]
-                energy = field[s, i, q]
-                if q < HALF:
-                    west = jnp.where(row < 2, halo_w[s, i, q], pltpu.roll(energy, 2, 0))
-                    flux = east_face * energy - west_face * west
-                else:
-                    east = jnp.where(row >= 6, halo_e[s, i, q - HALF], pltpu.roll(energy, 6, 0))
-                    flux = east_face * east - west_face * energy
-                energy = energy - float(COS[j]) * flux
-                if SIN[j] > 0:
-                    share = up_face * energy
-                    flux = share - shift_down(share)
-                else:
-                    share = down_face * energy
-                    flux = shift_up(share) - share
-                return energy - float(SIN[j]) * flux
-
-            def turned(q, here, following):
-                j = ORDER[q]
-                rate = turn_lat * float(COS_FACE[j]) + turn_depth * float(SIN_FACE[j])
-                return rate * jnp.where(rate > 0.0, here, following)
-
-            energies = [moved(q) for q in range(DIRS)]
-            fluxes = [turned(q, energies[q], energies[(q + 1) % DIRS]) for q in range(DIRS)]
-            for q in range(DIRS):
-                field[s + 1, i, q] = (energies[q] - (fluxes[q] - fluxes[q - 1])) * wet_here
+            west, mid, east, beside = ([coef[i, part, m] for m in range(6)] for part in range(4))
+            wet_here = from_lon(wets, 0)
+            wide = (west, mid, east)
+            narrow = (mid, beside)
+
+            def first_step(q):
+                parts = along_lon(q, (halo_w[i, q], field[i, q], halo_e[i, q]), wide, False)
+                return [along_lat(q, part, c) for part, c in zip(parts, wide)]
+
+            def second_step(q):
+                parts = along_lon(q, [one_on[part, q] for part in range(3)], wide, False)
+                parts = (parts[MID], jnp.where(row < 4, parts[EAST], parts[WEST]))
+                return [along_lat(q, part, c) for part, c in zip(parts, narrow)]
+
+            def third_step(q):
+                parts = along_lon(q, (two_on[0, q], two_on[1, q]), narrow, True)
+                return [along_lat(q, part, c) for part, c in zip(parts, narrow)]
+
+            def fourth_step(q):
+                parts = along_lon(q, (three_on[0, q], three_on[1, q]), narrow, True)
+                return [along_lat(q, parts[0], mid)]
+
+            def to(buffer):
+                def store(q, part, energy):
+                    buffer[part, q] = energy
+                return store
+
+            def to_back(q, part, energy):
+                back[pl.ds(n * DIRS + ORDER[q], 8, stride=ROWS), :] = energy * wet_here
+
+            refracted(first_step, wide, to(one_on))
+            refracted(second_step, narrow, to(two_on))
+            refracted(third_step, narrow, to(three_on))
+            refracted(fourth_step, (mid,), to_back)
             return 0
 
         lax.fori_loop(0, CHUNK, one, 0)
 
     def send_back(ch):
-        for n in range(CHUNK):
-            for q in range(DIRS):
-                back[pl.ds(n * DIRS + ORDER[q], 8, stride=ROWS), :] = field[NSUB, ch * CHUNK + n, q]
         for v in range(BLOCKS):
             blocks[v] = back[v * ROWS:(v + 1) * ROWS, :]
         for s in range(SOURCES):
@@ -308,28 +369,6 @@
                     ).start()
 
     def step(t, _):
-        def one(n, _):
-            s = NSUB - 1 - n
-            ch = t - 1 - s
-
-            @pl.when((ch >= 0) & (ch < CHUNKS))
-            def _():
-                for copy in halo_copies(ch, s):
-                    copy.wait_recv()
-                substep(ch, s)
-
-                @pl.when(s < NSUB - 1)
-                def _():
-                    send_halos(ch, s + 1)
-
-                @pl.when(s == NSUB - 1)
-                def _():
-                    send_back(ch)
-
-            return 0
-
-        lax.fori_loop(0, NSUB, one, 0)
-
         for ch in range(CHUNKS):
             @pl.when(t == ch)
             def _(ch=ch):
@@ -340,11 +379,18 @@
         @pl.when(t < CHUNKS)
         def _():
             source_terms(t)
-            send_halos(t, 0)
+            send_halos(t)
+
+        @pl.when(t >= 1)
+        def _():
+            for copy in halo_copies(t - 1):
+                copy.wait_recv()
+            propagate(t - 1)
+            send_back(t - 1)
 
         return 0
 
-    lax.fori_loop(0, CHUNKS + NSUB, step, 0)
+    lax.fori_loop(0, CHUNKS + 1, step, 0)
 
     wait_bytes(aux_in.at[0:SOURCES - 1], aux_send)
     for ch in range(CHUNKS):
@@ -352,61 +398,92 @@
         wait_bytes(outb.at[ch, 0:SOURCES - 1], out_send.at[ch])
 
     def drain(n, _):
-        for copy in halo_copies(lax.rem(n, CHUNKS), n // CHUNKS):
+        for copy in halo_copies(n):
             copy.wait_send()
         return 0
 
-    lax.fori_loop(0, CHUNKS * NSUB, drain, 0)
+    lax.fori_loop(0, CHUNKS, drain, 0)
     wait_bytes(out, out_recv)
+
+
+def finish(slots, moved, out, zeros, sems):
+    first = (lax.axis_index("comp") * REGIONS + lax.axis_index("lon")) * SLOTS
+    zeros[...] = jnp.zeros_like(zeros)
+    for k in range(SLOTS):
+        held = slots[first + k] >= 0
+
+        @pl.when(held)
+        def _(k=k):
+            pltpu.make_async_copy(moved.at[k], out.at[k], sems.at[k]).start()
+
+        @pl.when(jnp.logical_not(held))
+        def _(k=k):
+            pltpu.make_async_copy(zeros, out.at[k], sems.at[k]).start()
+
+    for k in range(SLOTS):
+        wait_bytes(out.at[k], sems.at[k])
 
 
 def per_device(spectra, wind_vectors, slot_block, wet_mask, depth_class):
     hbm = pl.BlockSpec(memory_space=pltpu.HBM)
+    vmem = pl.BlockSpec(memory_space=pltpu.VMEM)
     f32 = jnp.float32
     dma = pltpu.SemaphoreType.DMA
+    scratch = [
+        pltpu.VMEM((SLOTS, COMPS, POINTS), f32),
+        pltpu.VMEM((SLOTS, 2, POINTS), f32),
+        pltpu.SMEM((GROUPS * REGIONS * SLOTS,), jnp.int32),
+        pltpu.VMEM((GRID_LON, 2 * POINTS), jnp.int32),
+        pltpu.VMEM((2, GRID_LON), jnp.int32),
+        pltpu.SMEM((T_SIZE,), f32),
+        pltpu.VMEM((2, 8, POINTS), f32),
+        pltpu.VMEM((SLOTS, 8, POINTS), f32),
+        pltpu.VMEM((SOURCES, 8, POINTS), f32),
+        pltpu.VMEM((3, 8, POINTS), f32),
+        pltpu.VMEM((2, 32, POINTS), f32),
+        pltpu.VMEM((32, POINTS), f32),
+        pltpu.VMEM((GROUP_FREQS, 4, 6, 8, POINTS), f32),
+        pltpu.VMEM((BLOCKS * ROWS, POINTS), f32),
+        pltpu.VMEM((GROUP_FREQS, DIRS, 8, POINTS), f32),
+        pltpu.VMEM((GROUP_FREQS, DIRS, 8, POINTS), f32),
+        pltpu.VMEM((GROUP_FREQS, DIRS, 8, POINTS), f32),
+        pltpu.VMEM((3, DIRS, 8, POINTS), f32),
+        pltpu.VMEM((2, DIRS, 8, POINTS), f32),
+        pltpu.VMEM((2, DIRS, 8, POINTS), f32),
+        pltpu.VMEM((BLOCKS * ROWS, POINTS), f32),
+        pltpu.VMEM((BLOCKS, ROWS, POINTS), f32),
+        pltpu.VMEM((CHUNKS, SOURCES, ROWS, POINTS), f32),
+        dma((7,)),
+        dma((CHUNKS,)),
+        dma((CHUNKS,)),
+        dma,
+        dma,
+        dma((2, CHUNKS)),
+        dma((2, CHUNKS)),
+        dma((CHUNKS,)),
+        dma,
+    ] + [pltpu.VMEM((SOURCES, ROWS, POINTS), f32) for _ in range(CHUNKS)]
+    given = (spectra, wind_vectors, slot_block, wet_mask, depth_class.T, scalar_table(), latitude_table())
     moved = pl.pallas_call(
         kernel,
-        out_shape=jax.ShapeDtypeStruct((SLOTS, COMPS, POINTS), f32),
+        out_shape=pltpu.VMEM((SLOTS, COMPS, POINTS), f32),
         in_specs=[hbm] * 7,
-        out_specs=hbm,
-        scratch_shapes=[
-            pltpu.VMEM((SLOTS, COMPS, POINTS), f32),
-            pltpu.VMEM((SLOTS, 2, POINTS), f32),
-            pltpu.SMEM((GROUPS * REGIONS * SLOTS,), jnp.int32),
-            pltpu.VMEM((GRID_LON, 2 * POINTS), jnp.int32),
-            pltpu.VMEM((GRID_LON, 2), jnp.int32),
-            pltpu.SMEM((T_SIZE,), f32),
-            pltpu.VMEM((2, 8, POINTS), f32),
-            pltpu.VMEM((SLOTS, 8, POINTS), f32),
-            pltpu.VMEM((SOURCES, 8, POINTS), f32),
-            pltpu.VMEM((3, 8, POINTS), f32),
-            pltpu.VMEM((2, 3, 8, POINTS), f32),
-            pltpu.VMEM((GROUP_FREQS, 6, 8, POINTS), f32),
-            pltpu.VMEM((BLOCKS * ROWS, POINTS), f32),
-            pltpu.VMEM((NSUB + 1, GROUP_FREQS, DIRS, 8, POINTS), f32),
-            pltpu.VMEM((NSUB, GROUP_FREQS, HALF, 8, POINTS), f32),
-            pltpu.VMEM((NSUB, GROUP_FREQS, HALF, 8, POINTS), f32),
-            pltpu.VMEM((BLOCKS * ROWS, POINTS), f32),
-            pltpu.VMEM((BLOCKS, ROWS, POINTS), f32),
-            pltpu.VMEM((CHUNKS, SOURCES, ROWS, POINTS), f32),
-            dma((7,)),
-            dma((CHUNKS,)),
-            dma((CHUNKS,)),
-            dma,
-            dma,
-            dma((2, NSUB, CHUNKS)),
-            dma((2, NSUB, CHUNKS)),
-            dma((CHUNKS,)),
-            dma,
-        ] + [pltpu.VMEM((SOURCES, ROWS, POINTS), f32) for _ in range(CHUNKS)],
+        out_specs=vmem,
+        scratch_shapes=scratch,
         compiler_params=pltpu.CompilerParams(
-            collective_id=0, has_side_effects=True, vmem_limit_bytes=62 * 1024 * 1024
+            collective_id=0, has_side_effects=True, vmem_limit_bytes=40 * 1024 * 1024
         ),
         name="wave_step",
-    )(spectra, wind_vectors, slot_block, wet_mask, depth_class, scalar_table(), latitude_table())
-    first = (lax.axis_index("comp") * REGIONS + lax.axis_index("lon")) * SLOTS
-    mine = lax.dynamic_slice_in_dim(slot_block, first, SLOTS)
-    return jnp.where(mine[:, None, None] >= 0, moved, 0.0)
+    )(*[pltpu.with_memory_space_constraint(jnp.asarray(array), pltpu.HBM) for array in given])
+    return pl.pallas_call(
+        finish,
+        out_shape=jax.ShapeDtypeStruct((SLOTS, COMPS, POINTS), f32),
+        in_specs=[pl.BlockSpec(memory_space=pltpu.SMEM), vmem],
+        out_specs=hbm,
+        scratch_shapes=[pltpu.VMEM((COMPS, POINTS), f32), dma((SLOTS,))],
+        compiler_params=pltpu.CompilerParams(vmem_limit_bytes=8 * 1024 * 1024),
+        name="finish",
+    )(slot_block, pltpu.with_memory_space_constraint(moved, pltpu.VMEM))
 
 
 def solution(mesh):

time: 103 us -> 84.6 us (0.82)
  the two profiles are of different devices: /device:TPU:1 before, /device:TPU:0 now
where the time goes in v1:
time: 84.6 us; the launch traced here: 84.5 us
  Pallas kernels  84.5 us (100%)
    pallas_call x1, Pallas kernels, per_device(): pl.pallas_call(kernel, out_shape=pltpu.VMEM((SLOTS, COMPS, POINTS), f32),...  82.4 us
    pallas_call x1, Pallas kernels, per_device(): pl.pallas_call(finish, out_shape=jax.ShapeDtypeStruct((SLOTS, COMPS, POIN...  2.13 us

profile of v1, /device:TPU:0, one launch (start us, length us, event | category | flops | bytes accessed | tf_op | source)
XLA Modules:
  0.0 84.5 jit_solution(16971529336961262675)
XLA Ops:
  0.0 0.0 copy-start
  0.0 82.4 %wave_step.1.moved = f32[3,1728,128]{2,1,0:T(8,128)S(1)} custom-call(f32[3,1728,128]{2,1,0:T(8,128)} %x.1, f32[3,2,128]{2,1,0:T(2,128)} %wind.1, s32[384]{0:T(512)} %slots.3, s32[128,256]{1,0:T(8,128)} %wet.1, s32[2,128]{1,0:T(2,128)} %bitcast.1, f32[640]{0:T(1024)} %constant.4.clone.table, f32[2,8,128]{2,1,0:T(8,128)} %constant.5.clone.lat), custom_call_target="tpu_custom_call" | custom-call | tf_op jit(solution)/shard_map/wave_step/pallas_call | solution.py:467
  82.4 0.0 copy-done
  82.4 2.1 %finish.1 = f32[3,1728,128]{2,1,0:T(8,128)} custom-call(s32[384]{0:T(512)S(1)} %copy-done, f32[3,1728,128]{2,1,0:T(8,128)S(1)} %wave_step.1.moved), custom_call_target="tpu_custom_call" | custom-call | tf_op jit(solution)/shard_map/finish/pallas_call | solution.py:478
Async XLA Ops:
  0.0 82.4 %copy-start = (s32[384]{0:T(512)S(1)}, s32[384]{0:T(512)}, u32[]{:S(2)}) copy-start(s32[384]{0:T(512)} %slots.3) | copy-start | bytes 4612

commit v2 on v1

--- a/solution.py
+++ b/solution.py
@@ -47,6 +47,8 @@
 T_WEIGHT = T_SQUARE + FREQS
 T_WEIGHT_FREQ = T_WEIGHT + FREQS
 T_SIZE = 640
+LAG = 2
+WINDOW = 3
 
 WEST, MID, EAST, BESIDE = range(4)
 
@@ -114,7 +116,7 @@
                 )
     pl.semaphore_wait(barrier, SOURCES - 1)
 
-    for ch in range(CHUNKS):
+    def send_in(ch):
         for dg in (2, 1, 3, 0):
             to = lax.rem(me_c + dg, GROUPS)
             for k in range(SLOTS):
@@ -126,6 +128,9 @@
                     pltpu.make_async_remote_copy(
                         src, dst, in_send.at[ch], in_recv.at[ch], device_id=(to, region(k - 1)), device_id_type=MESH
                     ).start()
+
+    for ch in range(min(WINDOW, CHUNKS)):
+        send_in(ch)
 
     row = lax.broadcasted_iota(jnp.int32, (8, POINTS), 0)
     lane = lax.broadcasted_iota(jnp.int32, (8, POINTS), 1)
@@ -227,6 +232,7 @@
             found = jnp.where(held[s] == v, jnp.int32(s), found)
         holder.append(found)
     back_row = [jnp.maximum(h, 0) for h in held]
+    kept = [jnp.where(h >= 0, jnp.float32(1.0), jnp.float32(0.0)) for h in held]
 
     wait_bytes(aux_in, aux_recv)
     for v in range(BLOCKS):
@@ -355,7 +361,7 @@
         for v in range(BLOCKS):
             blocks[v] = back[v * ROWS:(v + 1) * ROWS, :]
         for s in range(SOURCES):
-            outb[ch, s] = blocks[back_row[s]]
+            outb[ch, s] = blocks[back_row[s]] * kept[s]
         for dg in (2, 1, 3, 0):
             to = lax.rem(me_c + dg, GROUPS)
             for k in range(SLOTS):
@@ -373,6 +379,9 @@
             @pl.when(t == ch)
             def _(ch=ch):
                 wait_bytes(inb[ch], in_recv.at[ch])
+                if ch + WINDOW < CHUNKS:
+                    wait_bytes(inb[ch].at[0:SOURCES - 1], in_send.at[ch])
+                    send_in(ch + WINDOW)
                 for v in range(BLOCKS):
                     ordered[v * ROWS:(v + 1) * ROWS, :] = inb[ch][holder[v]]
 
@@ -381,20 +390,21 @@
             source_terms(t)
             send_halos(t)
 
-        @pl.when(t >= 1)
+        @pl.when(t >= LAG)
         def _():
-            for copy in halo_copies(t - 1):
+            for copy in halo_copies(t - LAG):
                 copy.wait_recv()
-            propagate(t - 1)
-            send_back(t - 1)
+            propagate(t - LAG)
+            send_back(t - LAG)
 
         return 0
 
-    lax.fori_loop(0, CHUNKS + 1, step, 0)
+    lax.fori_loop(0, CHUNKS + LAG, step, 0)
 
     wait_bytes(aux_in.at[0:SOURCES - 1], aux_send)
     for ch in range(CHUNKS):
-        wait_bytes(inb[ch].at[0:SOURCES - 1], in_send.at[ch])
+        if ch + WINDOW >= CHUNKS:
+            wait_bytes(inb[ch].at[0:SOURCES - 1], in_send.at[ch])
         wait_bytes(outb.at[ch, 0:SOURCES - 1], out_send.at[ch])
 
     def drain(n, _):
@@ -406,22 +416,12 @@
     wait_bytes(out, out_recv)
 
 
-def finish(slots, moved, out, zeros, sems):
-    first = (lax.axis_index("comp") * REGIONS + lax.axis_index("lon")) * SLOTS
-    zeros[...] = jnp.zeros_like(zeros)
-    for k in range(SLOTS):
-        held = slots[first + k] >= 0
-
-        @pl.when(held)
-        def _(k=k):
-            pltpu.make_async_copy(moved.at[k], out.at[k], sems.at[k]).start()
-
-        @pl.when(jnp.logical_not(held))
-        def _(k=k):
-            pltpu.make_async_copy(zeros, out.at[k], sems.at[k]).start()
-
-    for k in range(SLOTS):
-        wait_bytes(out.at[k], sems.at[k])
+def finish(moved, out, sems):
+    copies = [pltpu.make_async_copy(moved.at[k], out.at[k], sems.at[k]) for k in range(SLOTS)]
+    for copy in copies:
+        copy.start()
+    for copy in copies:
+        copy.wait()
 
 
 def per_device(spectra, wind_vectors, slot_block, wet_mask, depth_class):
@@ -478,12 +478,12 @@
     return pl.pallas_call(
         finish,
         out_shape=jax.ShapeDtypeStruct((SLOTS, COMPS, POINTS), f32),
-        in_specs=[pl.BlockSpec(memory_space=pltpu.SMEM), vmem],
+        in_specs=[vmem],
         out_specs=hbm,
-        scratch_shapes=[pltpu.VMEM((COMPS, POINTS), f32), dma((SLOTS,))],
+        scratch_shapes=[dma((SLOTS,))],
         compiler_params=pltpu.CompilerParams(vmem_limit_bytes=8 * 1024 * 1024),
         name="finish",
-    )(slot_block, pltpu.with_memory_space_constraint(moved, pltpu.VMEM))
+    )(pltpu.with_memory_space_constraint(moved, pltpu.VMEM))
 
 
 def solution(mesh):

time: 84.6 us -> 71.5 us (0.85)
  the two profiles are of different devices: /device:TPU:0 before, /device:TPU:1 now
where the time goes in v2:
time: 71.5 us; the launch traced here: 71.4 us
  Pallas kernels  71.4 us (100%)
    pallas_call x1, Pallas kernels, per_device(): pl.pallas_call(kernel, out_shape=pltpu.VMEM((SLOTS, COMPS, POINTS), f32),...  69.9 us
    pallas_call x1, Pallas kernels, per_device(): pl.pallas_call(finish, out_shape=jax.ShapeDtypeStruct((SLOTS, COMPS, POIN...  1.52 us

profile of v2, /device:TPU:1, one launch (start us, length us, event | category | flops | bytes accessed | tf_op | source)
XLA Modules:
  0.0 71.4 jit_solution(12618773852333929397)
XLA Ops:
  0.0 69.9 %wave_step.1.moved = f32[3,1728,128]{2,1,0:T(8,128)S(1)} custom-call(f32[3,1728,128]{2,1,0:T(8,128)} %x.1, f32[3,2,128]{2,1,0:T(2,128)} %wind.1, s32[384]{0:T(512)} %slots.1, s32[128,256]{1,0:T(8,128)} %wet.1, s32[2,128]{1,0:T(2,128)} %bitcast.1, f32[640]{0:T(1024)} %constant.4.clone.table, f32[2,8,128]{2,1,0:T(8,128)} %constant.5.clone.lat), custom_call_target="tpu_custom_call" | custom-call | tf_op jit(solution)/shard_map/wave_step/pallas_call | solution.py:467
  69.9 1.5 %finish.1 = f32[3,1728,128]{2,1,0:T(8,128)} custom-call(f32[3,1728,128]{2,1,0:T(8,128)S(1)} %wave_step.1.moved), custom_call_target="tpu_custom_call" | custom-call | tf_op jit(solution)/shard_map/finish/pallas_call | solution.py:478

commit v3 on v2

--- a/solution.py
+++ b/solution.py
@@ -89,7 +89,7 @@
     x, wind, slots, wet, depth, table, lat, out,
     xv, windv, slot_s, wetv, depthv, table_s, latv,
     aux_out, aux_in, scal, cells, speeds, coef, ordered, field, halo_w, halo_e, one_on, two_on, three_on, back, blocks, outb,
-    local_sem, in_send, in_recv, aux_send, aux_recv, halo_send, halo_recv, out_send, out_recv,
+    local_sem, in_send, in_recv, aux_send, aux_recv, halo_send, halo_recv, out_send, out_recv, ready,
     *inb,
 ):
     me_c = lax.axis_index("comp")
@@ -97,6 +97,9 @@
 
     def region(shift):
         return lax.rem(me_r + (shift + REGIONS), REGIONS)
+
+    def across(dg):
+        return lax.rem(me_c + jnp.where(lax.rem(me_r, 2) == 0, dg, (GROUPS - dg) % GROUPS), GROUPS)
 
     loads = [
         pltpu.make_async_copy(src, dst, local_sem.at[n])
@@ -104,22 +107,21 @@
             ((x, xv), (wind, windv), (slots, slot_s), (wet, wetv), (depth, depthv), (table, table_s), (lat, latv))
         )
     ]
-    for load in loads:
-        load.start()
-
     barrier = pltpu.get_barrier_semaphore()
     for dg in range(GROUPS):
         for dr in (-1, 0, 1):
-            if dg or dr:
+            if (dg == 0) != (dr == 0):
                 pl.semaphore_signal(
                     barrier, inc=1, device_id=(lax.rem(me_c + dg, GROUPS), region(dr)), device_id_type=MESH
                 )
-    pl.semaphore_wait(barrier, SOURCES - 1)
-
-    def send_in(ch):
-        for dg in (2, 1, 3, 0):
-            to = lax.rem(me_c + dg, GROUPS)
-            for k in range(SLOTS):
+    for load in loads:
+        load.start()
+    pl.semaphore_wait(barrier, GROUPS + 1)
+
+    def send_in(ch, slots=(0, 2, 1)):
+        for k, dg in [(k, dg) for k in slots for dg in (1, 2, 3, 0)]:
+            to = across(dg)
+            if True:
                 src = x.at[k, pl.ds(to * GROUP_COMPS + ch * ROWS, ROWS)]
                 dst = inb[ch].at[me_c * SLOTS + k]
                 if dg == 0 and k == 1:
@@ -129,8 +131,13 @@
                         src, dst, in_send.at[ch], in_recv.at[ch], device_id=(to, region(k - 1)), device_id_type=MESH
                     ).start()
 
+    for dg in range(1, GROUPS):
+        pl.semaphore_signal(ready, inc=1, device_id=(lax.rem(me_c + dg, GROUPS), me_r), device_id_type=MESH)
     for ch in range(min(WINDOW, CHUNKS)):
-        send_in(ch)
+        send_in(ch, (1,))
+    pl.semaphore_wait(ready, GROUPS - 1)
+    for ch in range(min(WINDOW, CHUNKS)):
+        send_in(ch, (0, 2))
 
     row = lax.broadcasted_iota(jnp.int32, (8, POINTS), 0)
     lane = lax.broadcasted_iota(jnp.int32, (8, POINTS), 1)
@@ -362,9 +369,9 @@
             blocks[v] = back[v * ROWS:(v + 1) * ROWS, :]
         for s in range(SOURCES):
             outb[ch, s] = blocks[back_row[s]] * kept[s]
-        for dg in (2, 1, 3, 0):
-            to = lax.rem(me_c + dg, GROUPS)
-            for k in range(SLOTS):
+        for k, dg in [(k, dg) for k in (0, 2, 1) for dg in (1, 2, 3, 0)]:
+            to = across(dg)
+            if True:
                 src = outb.at[ch, to * SLOTS + k]
                 dst = out.at[k, pl.ds(me_c * GROUP_COMPS + ch * ROWS, ROWS)]
                 if dg == 0 and k == 1:
@@ -378,10 +385,10 @@
         for ch in range(CHUNKS):
             @pl.when(t == ch)
             def _(ch=ch):
-                wait_bytes(inb[ch], in_recv.at[ch])
                 if ch + WINDOW < CHUNKS:
                     wait_bytes(inb[ch].at[0:SOURCES - 1], in_send.at[ch])
                     send_in(ch + WINDOW)
+                wait_bytes(inb[ch], in_recv.at[ch])
                 for v in range(BLOCKS):
                     ordered[v * ROWS:(v + 1) * ROWS, :] = inb[ch][holder[v]]
 
@@ -462,6 +469,7 @@
         dma((2, CHUNKS)),
         dma((CHUNKS,)),
         dma,
+        pltpu.SemaphoreType.REGULAR,
     ] + [pltpu.VMEM((SOURCES, ROWS, POINTS), f32) for _ in range(CHUNKS)]
     given = (spectra, wind_vectors, slot_block, wet_mask, depth_class.T, scalar_table(), latitude_table())
     moved = pl.pallas_call(

time: 71.5 us -> 68.9 us (0.964)
  Pallas kernels: 71.4 us -> 68.8 us
    pallas_call x1, Pallas kernels: 69.9 us -> 67.3 us  [per_device(): pl.pallas_call(kernel, out_shape=pltpu.VMEM((SLOTS, COMPS, POINTS), f32),...]
where the time goes in v3:
time: 68.9 us; the launch traced here: 68.8 us
  Pallas kernels  68.8 us (100%)
    pallas_call x1, Pallas kernels, per_device(): pl.pallas_call(kernel, out_shape=pltpu.VMEM((SLOTS, COMPS, POINTS), f32),...  67.3 us
    pallas_call x1, Pallas kernels, per_device(): pl.pallas_call(finish, out_shape=jax.ShapeDtypeStruct((SLOTS, COMPS, POIN...  1.52 us

profile of v3, /device:TPU:1, one launch (start us, length us, event | category | flops | bytes accessed | tf_op | source)
XLA Modules:
  0.0 68.8 jit_solution(14330384514041186699)
XLA Ops:
  0.0 67.3 %wave_step.1.moved = f32[3,1728,128]{2,1,0:T(8,128)S(1)} custom-call(f32[3,1728,128]{2,1,0:T(8,128)} %x.1, f32[3,2,128]{2,1,0:T(2,128)} %wind.1, s32[384]{0:T(512)} %slots.1, s32[128,256]{1,0:T(8,128)} %wet.1, s32[2,128]{1,0:T(2,128)} %bitcast.1, f32[640]{0:T(1024)} %constant.4.clone.table, f32[2,8,128]{2,1,0:T(8,128)} %constant.5.clone.lat), custom_call_target="tpu_custom_call" | custom-call | tf_op jit(solution)/shard_map/wave_step/pallas_call | solution.py:475
  67.3 1.5 %finish.1 = f32[3,1728,128]{2,1,0:T(8,128)} custom-call(f32[3,1728,128]{2,1,0:T(8,128)S(1)} %wave_step.1.moved), custom_call_target="tpu_custom_call" | custom-call | tf_op jit(solution)/shard_map/finish/pallas_call | solution.py:486

commit v4 on v3

--- a/solution.py
+++ b/solution.py
@@ -133,11 +133,13 @@
 
     for dg in range(1, GROUPS):
         pl.semaphore_signal(ready, inc=1, device_id=(lax.rem(me_c + dg, GROUPS), me_r), device_id_type=MESH)
-    for ch in range(min(WINDOW, CHUNKS)):
+    for ch in range(2):
         send_in(ch, (1,))
     pl.semaphore_wait(ready, GROUPS - 1)
-    for ch in range(min(WINDOW, CHUNKS)):
+    for ch in range(2):
         send_in(ch, (0, 2))
+    for ch in range(2, 2):
+        send_in(ch)
 
     row = lax.broadcasted_iota(jnp.int32, (8, POINTS), 0)
     lane = lax.broadcasted_iota(jnp.int32, (8, POINTS), 1)
@@ -160,7 +162,7 @@
         total = jnp.sum(total, axis=0, keepdims=True)
         moment = jnp.sum(moment, axis=0, keepdims=True)
         mean = moment / (total + 1e-6)
-        aux_out[k] = zero
+        aux_out[k, 3:4, :] = zero[0:1]
         aux_out[k, 0:2, :] = windv[k]
         aux_out[k, 2:3, :] = 0.3 * (total / (total + 1.0)) / (mean * mean)
 
@@ -174,6 +176,9 @@
                 pltpu.make_async_remote_copy(
                     aux_out.at[k], dst, aux_send, aux_recv, device_id=(to, region(k - 1)), device_id_type=MESH
                 ).start()
+
+    for ch in range(2, WINDOW):
+        send_in(ch)
 
     for n in range(16):
         lon = lax.rem(me_r * REGION_LONS + (n - 6 + GRID_LON), GRID_LON)
@@ -241,11 +246,6 @@
     back_row = [jnp.maximum(h, 0) for h in held]
     kept = [jnp.where(h >= 0, jnp.float32(1.0), jnp.float32(0.0)) for h in held]
 
-    wait_bytes(aux_in, aux_recv)
-    for v in range(BLOCKS):
-        for n in range(3):
-            scal[n, v:v + 1, :] = aux_in[holder[v]][n:n + 1, :]
-
     def halo_copies(ch):
         freqs = pl.ds(ch * CHUNK, CHUNK)
         return [
@@ -391,6 +391,11 @@
                 wait_bytes(inb[ch], in_recv.at[ch])
                 for v in range(BLOCKS):
                     ordered[v * ROWS:(v + 1) * ROWS, :] = inb[ch][holder[v]]
+                if ch == 0:
+                    wait_bytes(aux_in, aux_recv)
+                    for v in range(BLOCKS):
+                        for n in range(3):
+                            scal[n, v:v + 1, :] = aux_in[holder[v]][n:n + 1, :]
 
         @pl.when(t < CHUNKS)
         def _():
@@ -444,20 +449,20 @@
         pltpu.VMEM((2, GRID_LON), jnp.int32),
         pltpu.SMEM((T_SIZE,), f32),
         pltpu.VMEM((2, 8, POINTS), f32),
-        pltpu.VMEM((SLOTS, 8, POINTS), f32),
-        pltpu.VMEM((SOURCES, 8, POINTS), f32),
+        pltpu.VMEM((SLOTS, 4, POINTS), f32),
+        pltpu.VMEM((SOURCES, 4, POINTS), f32),
         pltpu.VMEM((3, 8, POINTS), f32),
         pltpu.VMEM((2, 32, POINTS), f32),
         pltpu.VMEM((32, POINTS), f32),
         pltpu.VMEM((GROUP_FREQS, 4, 6, 8, POINTS), f32),
-        pltpu.VMEM((BLOCKS * ROWS, POINTS), f32),
+        pltpu.VMEM(((BLOCKS + 1) * ROWS, POINTS), f32),
         pltpu.VMEM((GROUP_FREQS, DIRS, 8, POINTS), f32),
         pltpu.VMEM((GROUP_FREQS, DIRS, 8, POINTS), f32),
         pltpu.VMEM((GROUP_FREQS, DIRS, 8, POINTS), f32),
         pltpu.VMEM((3, DIRS, 8, POINTS), f32),
         pltpu.VMEM((2, DIRS, 8, POINTS), f32),
         pltpu.VMEM((2, DIRS, 8, POINTS), f32),
-        pltpu.VMEM((BLOCKS * ROWS, POINTS), f32),
+        pltpu.VMEM(((BLOCKS + 1) * ROWS, POINTS), f32),
         pltpu.VMEM((BLOCKS, ROWS, POINTS), f32),
         pltpu.VMEM((CHUNKS, SOURCES, ROWS, POINTS), f32),
         dma((7,)),

time: 68.9 us -> 66 us (0.958)
  Pallas kernels: 68.8 us -> 65.9 us
    pallas_call x1, Pallas kernels: 67.3 us -> 64.4 us  [per_device(): pl.pallas_call(kernel, out_shape=pltpu.VMEM((SLOTS, COMPS, POINTS), f32),...]
where the time goes in v4:
time: 66 us; the launch traced here: 65.9 us
  Pallas kernels  65.9 us (100%)
    pallas_call x1, Pallas kernels, per_device(): pl.pallas_call(kernel, out_shape=pltpu.VMEM((SLOTS, COMPS, POINTS), f32),...  64.4 us
    pallas_call x1, Pallas kernels, per_device(): pl.pallas_call(finish, out_shape=jax.ShapeDtypeStruct((SLOTS, COMPS, POIN...  1.52 us

profile of v4, /device:TPU:1, one launch (start us, length us, event | category | flops | bytes accessed | tf_op | source)
XLA Modules:
  0.0 65.9 jit_solution(1217506204333429459)
XLA Ops:
  0.0 64.4 %wave_step.1.moved = f32[3,1728,128]{2,1,0:T(8,128)S(1)} custom-call(f32[3,1728,128]{2,1,0:T(8,128)} %x.1, f32[3,2,128]{2,1,0:T(2,128)} %wind.1, s32[384]{0:T(512)} %slots.1, s32[128,256]{1,0:T(8,128)} %wet.1, s32[2,128]{1,0:T(2,128)} %bitcast.1, f32[640]{0:T(1024)} %constant.4.clone.table, f32[2,8,128]{2,1,0:T(8,128)} %constant.5.clone.lat), custom_call_target="tpu_custom_call" | custom-call | tf_op jit(solution)/shard_map/wave_step/pallas_call | solution.py:480
  64.4 1.5 %finish.1 = f32[3,1728,128]{2,1,0:T(8,128)} custom-call(f32[3,1728,128]{2,1,0:T(8,128)S(1)} %wave_step.1.moved), custom_call_target="tpu_custom_call" | custom-call | tf_op jit(solution)/shard_map/finish/pallas_call | solution.py:491

commit v5 on v4

--- a/solution.py
+++ b/solution.py
@@ -49,6 +49,7 @@
 T_SIZE = 640
 LAG = 2
 WINDOW = 3
+EARLY = 2
 
 WEST, MID, EAST, BESIDE = range(4)
 
@@ -89,7 +90,7 @@
     x, wind, slots, wet, depth, table, lat, out,
     xv, windv, slot_s, wetv, depthv, table_s, latv,
     aux_out, aux_in, scal, cells, speeds, coef, ordered, field, halo_w, halo_e, one_on, two_on, three_on, back, blocks, outb,
-    local_sem, in_send, in_recv, aux_send, aux_recv, halo_send, halo_recv, out_send, out_recv, ready,
+    local_sem, in_send, in_recv, aux_send, aux_recv, halo_send, halo_recv, out_send, out_recv, ready, far,
     *inb,
 ):
     me_c = lax.axis_index("comp")
@@ -107,16 +108,23 @@
             ((x, xv), (wind, windv), (slots, slot_s), (wet, wetv), (depth, depthv), (table, table_s), (lat, latv))
         )
     ]
+    odd = lax.rem(me_r, 2)
+    beside_r = me_r + 1 - 2 * odd
+    beyond_r = region(2 * odd - 1)
+    leader = me_c == GROUPS - 1
+
     barrier = pltpu.get_barrier_semaphore()
-    for dg in range(GROUPS):
-        for dr in (-1, 0, 1):
-            if (dg == 0) != (dr == 0):
-                pl.semaphore_signal(
-                    barrier, inc=1, device_id=(lax.rem(me_c + dg, GROUPS), region(dr)), device_id_type=MESH
-                )
+    for dg in range(1, GROUPS):
+        pl.semaphore_signal(barrier, inc=1, device_id=(lax.rem(me_c + dg, GROUPS), me_r), device_id_type=MESH)
+    pl.semaphore_signal(barrier, inc=1, device_id=(me_c, beside_r), device_id_type=MESH)
+
+    @pl.when(leader)
+    def _():
+        pl.semaphore_signal(barrier, inc=1, device_id=(me_c, beyond_r), device_id_type=MESH)
+
     for load in loads:
         load.start()
-    pl.semaphore_wait(barrier, GROUPS + 1)
+    pl.semaphore_wait(barrier, jnp.where(leader, GROUPS + 1, GROUPS))
 
     def send_in(ch, slots=(0, 2, 1)):
         for k, dg in [(k, dg) for k in slots for dg in (1, 2, 3, 0)]:
@@ -124,22 +132,29 @@
             if True:
                 src = x.at[k, pl.ds(to * GROUP_COMPS + ch * ROWS, ROWS)]
                 dst = inb[ch].at[me_c * SLOTS + k]
-                if dg == 0 and k == 1:
+                if dg == 0 and isinstance(k, int) and k == 1:
                     pltpu.make_async_copy(src, dst, in_recv.at[ch]).start()
                 else:
                     pltpu.make_async_remote_copy(
                         src, dst, in_send.at[ch], in_recv.at[ch], device_id=(to, region(k - 1)), device_id_type=MESH
                     ).start()
 
+    @pl.when(leader)
+    def _():
+        pl.semaphore_signal(far, inc=1, device_id=(me_c, beyond_r), device_id_type=MESH)
+
     for dg in range(1, GROUPS):
         pl.semaphore_signal(ready, inc=1, device_id=(lax.rem(me_c + dg, GROUPS), me_r), device_id_type=MESH)
-    for ch in range(2):
+    for ch in range(EARLY):
         send_in(ch, (1,))
     pl.semaphore_wait(ready, GROUPS - 1)
-    for ch in range(2):
-        send_in(ch, (0, 2))
-    for ch in range(2, 2):
-        send_in(ch)
+    for ch in range(EARLY):
+        send_in(ch, (2 - 2 * odd,))
+    @pl.when(leader)
+    def _():
+        pl.semaphore_wait(far, 1)
+        for dg in range(1, GROUPS):
+            pl.semaphore_signal(far, inc=1, device_id=(lax.rem(me_c + dg, GROUPS), me_r), device_id_type=MESH)
 
     row = lax.broadcasted_iota(jnp.int32, (8, POINTS), 0)
     lane = lax.broadcasted_iota(jnp.int32, (8, POINTS), 1)
@@ -166,6 +181,13 @@
         aux_out[k, 0:2, :] = windv[k]
         aux_out[k, 2:3, :] = 0.3 * (total / (total + 1.0)) / (mean * mean)
 
+    @pl.when(jnp.logical_not(leader))
+    def _():
+        pl.semaphore_wait(far, 1)
+
+    for ch in range(EARLY):
+        send_in(ch, (2 * odd,))
+
     for dg in (2, 1, 3, 0):
         to = lax.rem(me_c + dg, GROUPS)
         for k in range(SLOTS):
@@ -177,7 +199,7 @@
                     aux_out.at[k], dst, aux_send, aux_recv, device_id=(to, region(k - 1)), device_id_type=MESH
                 ).start()
 
-    for ch in range(2, WINDOW):
+    for ch in range(EARLY, WINDOW):
         send_in(ch)
 
     for n in range(16):
@@ -475,6 +497,7 @@
         dma((CHUNKS,)),
         dma,
         pltpu.SemaphoreType.REGULAR,
+        pltpu.SemaphoreType.REGULAR,
     ] + [pltpu.VMEM((SOURCES, ROWS, POINTS), f32) for _ in range(CHUNKS)]
     given = (spectra, wind_vectors, slot_block, wet_mask, depth_class.T, scalar_table(), latitude_table())
     moved = pl.pallas_call(

time: 66 us -> 65.9 us (level)
  no operation moved by 1% of the time
where the time goes in v5:
time: 65.9 us; the launch traced here: 65.8 us
  Pallas kernels  65.8 us (100%)
    pallas_call x1, Pallas kernels, per_device(): pl.pallas_call(kernel, out_shape=pltpu.VMEM((SLOTS, COMPS, POINTS), f32),...  64.2 us
    pallas_call x1, Pallas kernels, per_device(): pl.pallas_call(finish, out_shape=jax.ShapeDtypeStruct((SLOTS, COMPS, POIN...  1.52 us

profile of v5, /device:TPU:1, one launch (start us, length us, event | category | flops | bytes accessed | tf_op | source)
XLA Modules:
  0.0 65.8 jit_solution(7455847269735461985)
XLA Ops:
  0.0 64.2 %wave_step.1.moved = f32[3,1728,128]{2,1,0:T(8,128)S(1)} custom-call(f32[3,1728,128]{2,1,0:T(8,128)} %x.1, f32[3,2,128]{2,1,0:T(2,128)} %wind.1, s32[384]{0:T(512)} %slots.1, s32[128,256]{1,0:T(8,128)} %wet.1, s32[2,128]{1,0:T(2,128)} %bitcast.1, f32[640]{0:T(1024)} %constant.4.clone.table, f32[2,8,128]{2,1,0:T(8,128)} %constant.5.clone.lat), custom_call_target="tpu_custom_call" | custom-call | tf_op jit(solution)/shard_map/wave_step/pallas_call | solution.py:503
  64.2 1.5 %finish.1 = f32[3,1728,128]{2,1,0:T(8,128)} custom-call(f32[3,1728,128]{2,1,0:T(8,128)S(1)} %wave_step.1.moved), custom_call_target="tpu_custom_call" | custom-call | tf_op jit(solution)/shard_map/finish/pallas_call | solution.py:514

commit v6 on v4

--- a/solution.py
+++ b/solution.py
@@ -369,7 +369,7 @@
             blocks[v] = back[v * ROWS:(v + 1) * ROWS, :]
         for s in range(SOURCES):
             outb[ch, s] = blocks[back_row[s]] * kept[s]
-        for k, dg in [(k, dg) for k in (0, 2, 1) for dg in (1, 2, 3, 0)]:
+        for k, dg in [(k, dg) for k in (2, 0, 1) for dg in (3, 2, 1, 0)]:
             to = across(dg)
             if True:
                 src = outb.at[ch, to * SLOTS + k]

time: 66 us -> 65.7 us (level)
  no operation moved by 1% of the time
where the time goes in v6:
time: 65.7 us; the launch traced here: 65.6 us
  Pallas kernels  65.6 us (100%)
    pallas_call x1, Pallas kernels, per_device(): pl.pallas_call(kernel, out_shape=pltpu.VMEM((SLOTS, COMPS, POINTS), f32),...  64.1 us
    pallas_call x1, Pallas kernels, per_device(): pl.pallas_call(finish, out_shape=jax.ShapeDtypeStruct((SLOTS, COMPS, POIN...  1.52 us

profile of v6, /device:TPU:1, one launch (start us, length us, event | category | flops | bytes accessed | tf_op | source)
XLA Modules:
  0.0 65.6 jit_solution(2595238529564625390)
XLA Ops:
  0.0 64.1 %wave_step.1.moved = f32[3,1728,128]{2,1,0:T(8,128)S(1)} custom-call(f32[3,1728,128]{2,1,0:T(8,128)} %x.1, f32[3,2,128]{2,1,0:T(2,128)} %wind.1, s32[384]{0:T(512)} %slots.1, s32[128,256]{1,0:T(8,128)} %wet.1, s32[2,128]{1,0:T(2,128)} %bitcast.1, f32[640]{0:T(1024)} %constant.4.clone.table, f32[2,8,128]{2,1,0:T(8,128)} %constant.5.clone.lat), custom_call_target="tpu_custom_call" | custom-call | tf_op jit(solution)/shard_map/wave_step/pallas_call | solution.py:480
  64.1 1.5 %finish.1 = f32[3,1728,128]{2,1,0:T(8,128)} custom-call(f32[3,1728,128]{2,1,0:T(8,128)S(1)} %wave_step.1.moved), custom_call_target="tpu_custom_call" | custom-call | tf_op jit(solution)/shard_map/finish/pallas_call | solution.py:491

commit v7 on v6

--- a/solution.py
+++ b/solution.py
@@ -135,12 +135,6 @@
         pl.semaphore_signal(ready, inc=1, device_id=(lax.rem(me_c + dg, GROUPS), me_r), device_id_type=MESH)
     for ch in range(2):
         send_in(ch, (1,))
-    pl.semaphore_wait(ready, GROUPS - 1)
-    for ch in range(2):
-        send_in(ch, (0, 2))
-    for ch in range(2, 2):
-        send_in(ch)
-
     row = lax.broadcasted_iota(jnp.int32, (8, POINTS), 0)
     lane = lax.broadcasted_iota(jnp.int32, (8, POINTS), 1)
 
@@ -165,6 +159,10 @@
         aux_out[k, 3:4, :] = zero[0:1]
         aux_out[k, 0:2, :] = windv[k]
         aux_out[k, 2:3, :] = 0.3 * (total / (total + 1.0)) / (mean * mean)
+
+    pl.semaphore_wait(ready, GROUPS - 1)
+    for ch in range(2):
+        send_in(ch, (0, 2))
 
     for dg in (2, 1, 3, 0):
         to = lax.rem(me_c + dg, GROUPS)

time: 65.7 us -> 65.7 us (level)
  no operation moved by 1% of the time
where the time goes in v7:
time: 65.7 us; the launch traced here: 65.6 us
  Pallas kernels  65.6 us (100%)
    pallas_call x1, Pallas kernels, per_device(): pl.pallas_call(kernel, out_shape=pltpu.VMEM((SLOTS, COMPS, POINTS), f32),...  64.1 us
    pallas_call x1, Pallas kernels, per_device(): pl.pallas_call(finish, out_shape=jax.ShapeDtypeStruct((SLOTS, COMPS, POIN...  1.52 us

profile of v7, /device:TPU:1, one launch (start us, length us, event | category | flops | bytes accessed | tf_op | source)
XLA Modules:
  0.0 65.6 jit_solution(7039426705815213981)
XLA Ops:
  0.0 64.1 %wave_step.1.moved = f32[3,1728,128]{2,1,0:T(8,128)S(1)} custom-call(f32[3,1728,128]{2,1,0:T(8,128)} %x.1, f32[3,2,128]{2,1,0:T(2,128)} %wind.1, s32[384]{0:T(512)} %slots.1, s32[128,256]{1,0:T(8,128)} %wet.1, s32[2,128]{1,0:T(2,128)} %bitcast.1, f32[640]{0:T(1024)} %constant.4.clone.table, f32[2,8,128]{2,1,0:T(8,128)} %constant.5.clone.lat), custom_call_target="tpu_custom_call" | custom-call | tf_op jit(solution)/shard_map/wave_step/pallas_call | solution.py:478
  64.1 1.5 %finish.1 = f32[3,1728,128]{2,1,0:T(8,128)} custom-call(f32[3,1728,128]{2,1,0:T(8,128)S(1)} %wave_step.1.moved), custom_call_target="tpu_custom_call" | custom-call | tf_op jit(solution)/shard_map/finish/pallas_call | solution.py:489

commit v8 on v7

--- a/solution.py
+++ b/solution.py
@@ -161,8 +161,6 @@
         aux_out[k, 2:3, :] = 0.3 * (total / (total + 1.0)) / (mean * mean)
 
     pl.semaphore_wait(ready, GROUPS - 1)
-    for ch in range(2):
-        send_in(ch, (0, 2))
 
     for dg in (2, 1, 3, 0):
         to = lax.rem(me_c + dg, GROUPS)
@@ -175,6 +173,8 @@
                     aux_out.at[k], dst, aux_send, aux_recv, device_id=(to, region(k - 1)), device_id_type=MESH
                 ).start()
 
+    for ch in range(2):
+        send_in(ch, (0, 2))
     for ch in range(2, WINDOW):
         send_in(ch)
 

time: 65.7 us -> 66.3 us (level)
  no operation moved by 1% of the time
where the time goes in v8:
time: 66.3 us; the launch traced here: 66.2 us
  Pallas kernels  66.2 us (100%)
    pallas_call x1, Pallas kernels, per_device(): pl.pallas_call(kernel, out_shape=pltpu.VMEM((SLOTS, COMPS, POINTS), f32),...  64.7 us
    pallas_call x1, Pallas kernels, per_device(): pl.pallas_call(finish, out_shape=jax.ShapeDtypeStruct((SLOTS, COMPS, POIN...  1.52 us

profile of v8, /device:TPU:1, one launch (start us, length us, event | category | flops | bytes accessed | tf_op | source)
XLA Modules:
  0.0 66.2 jit_solution(6887067766358561539)
XLA Ops:
  0.0 64.7 %wave_step.1.moved = f32[3,1728,128]{2,1,0:T(8,128)S(1)} custom-call(f32[3,1728,128]{2,1,0:T(8,128)} %x.1, f32[3,2,128]{2,1,0:T(2,128)} %wind.1, s32[384]{0:T(512)} %slots.1, s32[128,256]{1,0:T(8,128)} %wet.1, s32[2,128]{1,0:T(2,128)} %bitcast.1, f32[640]{0:T(1024)} %constant.4.clone.table, f32[2,8,128]{2,1,0:T(8,128)} %constant.5.clone.lat), custom_call_target="tpu_custom_call" | custom-call | tf_op jit(solution)/shard_map/wave_step/pallas_call | solution.py:478
  64.7 1.5 %finish.1 = f32[3,1728,128]{2,1,0:T(8,128)} custom-call(f32[3,1728,128]{2,1,0:T(8,128)S(1)} %wave_step.1.moved), custom_call_target="tpu_custom_call" | custom-call | tf_op jit(solution)/shard_map/finish/pallas_call | solution.py:489
